TPU v7x, 32 devices: a whole 2x2x4 slice. The times are simulated.
32 devices in a mesh: wide: 4 (over y, x), narrow: 8 (over z, core).
Axes of the slice: x: 2, y: 2, z: 4, core: 2. Of those that a mesh axis runs over, the one named last changes fastest.
Arguments:
- pair_integrals: bfloat16 [65536, 32], P(('wide', 'narrow')), may hold values from -0.0625 to 0.0625
- screening: bfloat16 [32, 32], replicated, may hold values from -1 to 1
- virtual_integrals: bfloat16 [32, 1024, 1024], P(('wide', 'narrow')), may hold values from -0.375 to 0.375
- trials: bfloat16 [1, 256, 1024], P(None, None, 'narrow'), may hold values from -6 to 6
Outputs:
- response: float32 [1024, 1, 256], P('narrow', None, 'wide')
All inputs are finite; a program needn't handle non-finite values.
Results may differ from a plain program's by a relative error of at most 0.0041.
Values may be sent and summed in bfloat16 or wider, within the bound.
A program may use at most 64 MiB of HBM per device.

v0:
```python
import jax
import jax.numpy as jnp
from jax import lax
from jax.sharding import PartitionSpec as P

O = 256


def per_device(pair_integrals, screening, virtual_integrals, trials):
    screened = jnp.dot(pair_integrals, screening, preferred_element_type=jnp.float32).astype(
        jnp.bfloat16
    )
    blocks = screened.reshape((1, 1) + screened.shape)
    owned_tiles = lax.all_to_all(
        lax.all_to_all(blocks, "wide", split_axis=3, concat_axis=0, tiled=True),
        "narrow",
        split_axis=3,
        concat_axis=1,
        tiled=True,
    )
    aux_here = owned_tiles.shape[3]
    pair_tiles = owned_tiles.reshape(O, O, aux_here)
    whole_trials = lax.all_gather(trials, "narrow", axis=2, tiled=True)
    halves = jnp.einsum(
        "qab,sjb->qasj", virtual_integrals, whole_trials, preferred_element_type=jnp.float32
    ).astype(jnp.bfloat16)
    shares = lax.psum_scatter(
        jnp.einsum("qasj,ijq->asi", halves, pair_tiles, preferred_element_type=jnp.float32),
        "narrow",
        scatter_dimension=0,
        tiled=True,
    )
    return lax.psum_scatter(shares, "wide", scatter_dimension=2, tiled=True)


def solution(mesh):
    return jax.shard_map(
        per_device,
        mesh=mesh,
        in_specs=(
            P(("wide", "narrow"), None),
            P(),
            P(("wide", "narrow"), None, None),
            P(None, None, "narrow"),
        ),
        out_specs=P("narrow", None, "wide"),
        check_vma=False,
    )
```

profile of v0, /device:TPU:0, one launch (start us, length us, event | category | flops | bytes accessed | tf_op | source)
XLA Modules:
  0.0 105.0 jit_solution(8428374430887655571)
XLA Ops:
  6.5 0.0 copy-start
  6.5 1.3 %fusion = bf16[1,1,2048,32]{2,3,1,0:T(8,128)(2,1)S(1)} fusion(bf16[2048,32]{0,1:T(8,128)(2,1)} %param.4, bf16[32,32]{1,0:T(8,128)(2,1)} %param.5), kind=kOutput, calls=%fused_computation.1 | convolution fusion | flops 4259840 | bytes 264192 | tf_op jit(solution)/shard_map/dot_general | solution.py:10
  7.8 0.2 copy.19
  8.0 0.5 broadcast
  8.6 1.4 %reduce = bf16[32,2048]{1,0:T(8,128)(2,1)S(1)} reduce(bf16[32,1,1,2048]{3,2,1,0:T(2,128)(2,1)S(1)} %bitcast.37, bf16[]{:T(256)} %broadcast), dimensions={1,2}, to_apply=%bitcast.36.reduce_sub_computation | reduce | bytes 262146
  9.9 0.2 reshape.24
  10.1 10.0 %all_to_all.33 = bf16[4,2,8192]{2,1,0:T(2,128)(2,1)S(1)} all-to-all(bf16[4,2,8192]{2,1,0:T(2,128)(2,1)S(1)} %reshape.24), channel_id=1, replica_groups=mesh['wide'=4,'narrow'=8] {'wide'}, dimensions={0} | all-to-all | bytes 262144 | tf_op jit(solution)/shard_map/all_to_all | solution.py:15
  20.1 0.1 reshape.25
  20.2 0.1 copy.18
  20.3 0.7 copy.11
  21.0 4.9 %all-to-all-start.1 = ((bf16[4,1,2048,8]{2,0,1,3:T(4,128)(2,1)}), bf16[4,1,2048,8]{2,0,1,3:T(4,128)(2,1)S(1)}, u32[]{:S(2)}, u32[]{:S(2)}) async-start(bf16[4,1,2048,8]{2,0,1,3:T(4,128)(2,1)} %copy.11), calls=%async_computation.1 | async-start | bytes 262144 | tf_op jit(solution)/shard_map/all_to_all | solution.py:14
  25.9 0.0 reduce-scatter.3.cloned.1.call-start
  26.0 15.5 %all_gather.3 = bf16[1,256,1024]{2,1,0:T(8,128)(2,1)S(1)} all-gather(bf16[1,256,128]{2,1,0:T(8,128)(2,1)S(1)} %copy-done.1), channel_id=1, replica_groups=mesh['wide'=4,'narrow'=8] {'narrow'}, dimensions={2}, use_global_device_ids=true | all-gather | bytes 589824 | tf_op jit(solution)/shard_map/all_gather | solution.py:23
  41.5 0.0 all-to-all-done.1
  41.5 0.1 copy.12
  41.6 0.1 reshape.23
  41.7 0.0 copy-done
  41.7 2.0 %convolution_bitcast_fusion = f32[1024,1,256]{2,0,1:T(8,128)} fusion(bf16[256,256]{1,0:T(8,128)(2,1)S(1)} %reshape.23, bf16[1,1024,1024]{2,1,0:T(8,128)(2,1)S(1)} %copy-done, bf16[1,256,1024]{2,1,0:T(8,128)(2,1)S(1)} %all_gather.3), kind=kOutput, calls=%fused_computation.4 | convolution fusion | flops 671350784 | bytes 3801088 | tf_op jit(solution)/shard_map/qasj,ijq->asi/dot_general | solution.py:28
  43.7 0.0 reduce-scatter.3.cloned.1.call-update
  43.7 0.0 reduce-scatter.5.cloned.1.call-start
  43.7 29.6 %reduce-scatter.3.cloned.1.call-done = f32[128,1,256]{2,0,1:T(8,128)} async-done(((f32[1024,1,256]{2,0,1:T(8,128)}), f32[128,1,256]{2,0,1:T(8,128)}) %reduce-scatter.3.cloned.1.call-update) | async-done | bytes 131088 | tf_op jit(solution)/shard_map/reduce_scatter | solution.py:27
  73.3 1.6 %copy.13 = f32[128,1,256]{0,1,2:T(1,128)} copy(f32[128,1,256]{2,0,1:T(8,128)} %reduce-scatter.3.cloned.1.call-done) | data formatting | bytes 262144 | tf_op jit(solution)/shard_map/reduce_scatter | solution.py:27
  74.9 0.0 reduce-scatter.5.cloned.1.call-update
  75.0 23.2 %reduce-scatter.5.cloned.1.call-done = f32[128,1,64]{0,1,2:T(1,128)} async-done(((f32[128,1,256]{0,1,2:T(1,128)}), f32[128,1,64]{0,1,2:T(1,128)}) %reduce-scatter.5.cloned.1.call-update) | async-done | bytes 32784 | tf_op jit(solution)/shard_map/reduce_scatter | solution.py:33
  (2 shorter events, 0.0 us)
Async XLA Ops:
  6.5 35.1 %copy-start = (bf16[1,1024,1024]{2,1,0:T(8,128)(2,1)S(1)}, bf16[1,1024,1024]{2,1,0:T(8,128)(2,1)}, u32[]{:S(2)}) copy-start(bf16[1,1024,1024]{2,1,0:T(8,128)(2,1)} %param.6) | copy-start | bytes 6291460
  6.5 19.4 %copy-start.1 = (bf16[1,256,128]{2,1,0:T(8,128)(2,1)S(1)}, bf16[1,256,128]{2,1,0:T(8,128)(2,1)}, u32[]{:S(2)}) copy-start(bf16[1,256,128]{2,1,0:T(8,128)(2,1)} %param.7) | copy-start | bytes 196612
  21.0 20.5 %all-to-all-start.1 = ((bf16[4,1,2048,8]{2,0,1,3:T(4,128)(2,1)}), bf16[4,1,2048,8]{2,0,1,3:T(4,128)(2,1)S(1)}, u32[]{:S(2)}, u32[]{:S(2)}) async-start(bf16[4,1,2048,8]{2,0,1,3:T(4,128)(2,1)} %copy.11), calls=%async_computation.1 | async-start | bytes 262144 | tf_op jit(solution)/shard_map/all_to_all | solution.py:14
  25.9 47.4 %reduce-scatter.3.cloned.1.call-start = ((), (), s32[]{:S(2)}) async-start(), calls=%async_computation.4 | async-start | bytes 1179648 | tf_op jit(solution)/shard_map/reduce_scatter | solution.py:27
  43.7 54.4 %reduce-scatter.5.cloned.1.call-start = ((), (), s32[]{:S(2)}) async-start(), calls=%async_computation.5 | async-start | bytes 163840 | tf_op jit(solution)/shard_map/reduce_scatter | solution.py:33
Sparse Core Ops, SparseCore 0:
  43.8 29.4 reduce-scatter.2
  76.0 22.0 reduce-scatter.4
where the time goes:
time: 105 us
  waiting for transfers between devices  52.8 us (50%)
  blocking collectives  25.5 us (24%)
  between operations  13.5 us (13%)
  starting transfers between devices  4.96 us (5%)
  local copies, waits for them, and re-layouts  3.6 us (3%)
  matrix products  3.27 us (3%)
  other arithmetic  1.38 us (1%)
    reduce_scatter x1, waiting for transfers between devices, per_device(): lax.psum_scatter(jnp.einsum('qasj,ijq->asi', halves, pair_tiles, preferre...  29.6 us
    reduce_scatter x1, waiting for transfers between devices, per_device(): return lax.psum_scatter(shares, 'wide', scatter_dimension=2, tiled=True)  23.2 us
    all_gather x1, blocking collectives, per_device(): whole_trials = lax.all_gather(trials, 'narrow', axis=2, tiled=True)  15.5 us
    all_to_all x1, blocking collectives, per_device(): lax.all_to_all(blocks, 'wide', split_axis=3, concat_axis=0, tiled=True)  9.99 us
    all_to_all x1, starting transfers between devices, per_device(): lax.all_to_all(lax.all_to_all(blocks, 'wide', split_axis=3, concat_axis=0...  4.88 us
  transfers between devices with their start and end apart: 3, of which 2 were waited for; matrix products, arithmetic and copies ran while one was open for 0% of the time, Pallas kernels for 0%

commit v1 on v0

--- a/solution.py
+++ b/solution.py
@@ -1,12 +1,225 @@
+import functools
+
 import jax
 import jax.numpy as jnp
 from jax import lax
+from jax.experimental import pallas as pl
+from jax.experimental.pallas import tpu as pltpu
 from jax.sharding import PartitionSpec as P
 
-O = 256
-
-
-def per_device(pair_integrals, screening, virtual_integrals, trials):
+LANES = 128
+CORES = 2
+MESH = pl.DeviceIdType.MESH
+
+
+def kernel(
+    wides, narrows, pairs_ref, screen_ref, virt_ref, trial_ref, out_ref,
+    pairs, screen, virt, trial, staged, tiles, tiles_wide, tiles_all, total, halves,
+    to_core, from_core, summed, to_wide, from_wide, to_z, from_z,
+    local_sem, send_sem, recv_sem,
+):
+    zs = narrows // CORES
+    w, n = lax.axis_index("wide"), lax.axis_index("narrow")
+    z, c = lax.div(n, CORES), lax.rem(n, CORES)
+    mate = 1 - c
+    orbitals = trial.shape[1]
+    cut = orbitals // wides
+    wide_at = [lax.rem(w + m, wides) for m in range(wides)]
+    z_at = [lax.rem(z + k, zs) for k in range(zs)]
+    z_from = [lax.rem(z + zs - k, zs) for k in range(zs)]
+    narrow_at = [lax.rem(n + m, narrows) for m in range(narrows)]
+
+    barrier = pltpu.get_barrier_semaphore()
+    for m in range(1, wides):
+        pl.semaphore_signal(barrier, inc=1, device_id={"wide": wide_at[m], "narrow": n}, device_id_type=MESH)
+    for m in range(1, narrows):
+        pl.semaphore_signal(barrier, inc=1, device_id={"wide": w, "narrow": narrow_at[m]}, device_id_type=MESH)
+
+    sent = []
+
+    def send(source, target, wide, narrow):
+        at = len(sent)
+        copy = pltpu.make_async_remote_copy(
+            src_ref=source, dst_ref=target, send_sem=send_sem.at[at], recv_sem=recv_sem.at[at],
+            device_id={"wide": wide, "narrow": narrow}, device_id_type=MESH,
+        )
+        copy.start()
+        sent.append(copy)
+        return copy
+
+    def fetch(source, target, at):
+        copy = pltpu.make_async_copy(source, target, local_sem.at[at])
+        copy.start()
+        return copy
+
+    get_pairs = fetch(pairs_ref, pairs, 0)
+    get_screen = fetch(screen_ref, screen, 1)
+    get_trial = fetch(trial_ref, trial.at[n], 2)
+    depth = virt.shape[2]
+    get_virt = [
+        fetch(virt_ref.at[:, pl.ds(pl.multiple_of(z_from[k] * depth, depth), depth)], virt.at[k], 3 + k)
+        for k in range(zs)
+    ]
+
+    get_pairs.wait()
+    get_screen.wait()
+    product = lax.dot_general(
+        screen[...], pairs[...], (((0,), (0,)), ((), ())), preferred_element_type=jnp.float32
+    )
+    aux = wides * narrows
+    rows = tiles.shape[2]
+    halves_j = orbitals // LANES
+    own_i = rows // halves_j
+    for i in range(own_i):
+        for h in range(halves_j):
+            t = i * halves_j + h
+            staged[pl.ds(h * own_i + i, aux, stride=rows), :] = product[:, t * LANES : (t + 1) * LANES]
+    tiles[...] = staged[...].reshape(tiles.shape).astype(jnp.bfloat16)
+    tiles_wide[w] = tiles[w]
+    get_trial.wait()
+
+    pl.semaphore_wait(barrier, wides + narrows - 2)
+
+    def share(block, of):
+        return trial.at[block, pl.ds(pl.multiple_of(of * cut, cut), cut)]
+
+    along_z = {k: send(share(n, w), share(n, w), w, z_at[k] * CORES + c) for k in range(zs - 1, 0, -1)}
+    to_mate = send(trial.at[n], trial.at[n], w, z * CORES + mate)
+    tiles_in = [send(tiles.at[wide_at[m]], tiles_wide.at[w], wide_at[m], n) for m in range(1, wides)]
+
+    def chunk(k):
+        first = z_from[k] * CORES
+        wide_rows = jnp.concatenate([trial[first + p] for p in range(CORES)], axis=1)
+        return lax.dot_general(
+            wide_rows, virt[k], (((1,), (1,)), ((), ())), preferred_element_type=jnp.float32
+        )
+
+    get_virt[0].wait()
+    to_mate.wait_recv()
+    total[...] = chunk(0)
+
+    across = {}
+    for k in range(1, zs):
+        along_z[k].wait_recv()
+        block = z_from[k] * CORES + c
+        across[k] = [send(share(block, w), share(block, w), wide_at[m], n) for m in range(1, wides)]
+
+    for copy in tiles_in:
+        copy.wait_recv()
+    tiles_all[n] = tiles_wide[:, n]
+    tiles_done = [
+        send(tiles_wide.at[:, narrow_at[m]], tiles_all.at[n], w, narrow_at[m]) for m in range(1, narrows)
+    ]
+
+    relayed = {}
+    for k in range(1, zs):
+        for copy in across[k]:
+            copy.wait_recv()
+        block = z_from[k] * CORES + c
+        relayed[k] = send(trial.at[block], trial.at[block], w, z * CORES + mate)
+    for k in range(1, zs):
+        get_virt[k].wait()
+        relayed[k].wait_recv()
+        total[...] += chunk(k)
+    for b in range(narrows):
+        halves[b] = total[:, b * LANES : (b + 1) * LANES].astype(jnp.bfloat16)
+
+    for copy in tiles_done:
+        copy.wait_recv()
+    columns = []
+    for h in range(halves_j):
+        parts = [
+            tiles_all[b, a].astype(jnp.float32)[h * own_i : (h + 1) * own_i]
+            for a in range(wides)
+            for b in range(narrows)
+        ]
+        columns.append(jnp.concatenate(parts, axis=0))
+    screened = jnp.concatenate(columns, axis=1).astype(jnp.bfloat16)
+
+    order = list(range(1, zs)) + [0]
+    from_mate, from_wides, from_zs = {}, {}, {}
+    for k in order:
+        to_core[k] = jnp.dot(
+            screened, halves[z_at[k] * CORES + mate], preferred_element_type=jnp.float32
+        ).astype(jnp.bfloat16)
+        from_mate[k] = send(to_core.at[k], from_core.at[k], w, z * CORES + mate)
+    for k in order:
+        own = jnp.dot(screened, halves[z_at[k] * CORES + c], preferred_element_type=jnp.float32)
+        from_mate[k].wait_recv()
+        value = own + from_core[k].astype(jnp.float32)
+        summed[k] = value
+        to_wide[k] = value.astype(jnp.bfloat16)
+        from_wides[k] = [
+            send(
+                to_wide.at[k, pl.ds(pl.multiple_of(wide_at[m] * cut, cut), cut)],
+                from_wide.at[k, m - 1], wide_at[m], n,
+            )
+            for m in range(1, wides)
+        ]
+    for k in order:
+        value = summed[k, pl.ds(pl.multiple_of(w * cut, cut), cut), :]
+        for m in range(1, wides):
+            from_wides[k][m - 1].wait_recv()
+            value = value + from_wide[k, m - 1].astype(jnp.float32)
+        if k:
+            to_z[k - 1] = value.astype(jnp.bfloat16)
+            from_zs[k] = send(to_z.at[k - 1], from_z.at[k - 1], w, z_at[k] * CORES + c)
+    for k in range(1, zs):
+        from_zs[k].wait_recv()
+        value = value + from_z[k - 1].astype(jnp.float32)
+    out_ref[...] = value
+    for copy in sent:
+        copy.wait_send()
+
+
+def fused(wides, narrows, pair_integrals, screening, virtual_integrals, trials):
+    zs = narrows // CORES
+    orbitals, columns = trials.shape[1:]
+    virtuals = virtual_integrals.shape[1]
+    aux = screening.shape[1]
+    pairs_here = pair_integrals.shape[0]
+    rows = pairs_here // LANES
+    cut = orbitals // wides
+    bf, f4 = jnp.bfloat16, jnp.float32
+    copies = (zs - 1) * 2 + 1 + (zs - 1) * (wides - 1) + (wides - 1) + (narrows - 1)
+    copies += zs + zs * (wides - 1) + (zs - 1)
+    anywhere = pl.BlockSpec(memory_space=pl.ANY)
+    out = pl.pallas_call(
+        functools.partial(kernel, wides, narrows),
+        out_shape=jax.ShapeDtypeStruct((cut, columns), f4),
+        in_specs=[anywhere] * 4,
+        out_specs=pl.BlockSpec(memory_space=pltpu.VMEM),
+        scratch_shapes=[
+            pltpu.VMEM((aux, pairs_here), bf),
+            pltpu.VMEM(screening.shape, bf),
+            pltpu.VMEM((zs, virtuals, virtuals // zs), bf),
+            pltpu.VMEM((narrows, orbitals, columns), bf),
+            pltpu.VMEM((aux * rows, LANES), f4),
+            pltpu.VMEM((wides, narrows, rows, LANES), bf),
+            pltpu.VMEM((wides, narrows, rows, LANES), bf),
+            pltpu.VMEM((narrows, wides, rows, LANES), bf),
+            pltpu.VMEM((orbitals, virtuals), f4),
+            pltpu.VMEM((narrows, orbitals, columns), bf),
+            pltpu.VMEM((zs, orbitals, columns), bf),
+            pltpu.VMEM((zs, orbitals, columns), bf),
+            pltpu.VMEM((zs, orbitals, columns), f4),
+            pltpu.VMEM((zs, orbitals, columns), bf),
+            pltpu.VMEM((zs, wides - 1, cut, columns), bf),
+            pltpu.VMEM((zs - 1, cut, columns), bf),
+            pltpu.VMEM((zs - 1, cut, columns), bf),
+            pltpu.SemaphoreType.DMA((3 + zs,)),
+            pltpu.SemaphoreType.DMA((copies,)),
+            pltpu.SemaphoreType.DMA((copies,)),
+        ],
+        compiler_params=pltpu.CompilerParams(
+            collective_id=0, has_side_effects=True, vmem_limit_bytes=48 * 2**20
+        ),
+    )(pair_integrals.T, screening, virtual_integrals[0], trials[0])
+    return out.T[:, None, :]
+
+
+def plain(pair_integrals, screening, virtual_integrals, trials):
+    orbitals = trials.shape[1]
     screened = jnp.dot(pair_integrals, screening, preferred_element_type=jnp.float32).astype(
         jnp.bfloat16
     )
@@ -18,8 +231,7 @@
         concat_axis=1,
         tiled=True,
     )
-    aux_here = owned_tiles.shape[3]
-    pair_tiles = owned_tiles.reshape(O, O, aux_here)
+    pair_tiles = owned_tiles.reshape(orbitals, orbitals, owned_tiles.shape[3])
     whole_trials = lax.all_gather(trials, "narrow", axis=2, tiled=True)
     halves = jnp.einsum(
         "qab,sjb->qasj", virtual_integrals, whole_trials, preferred_element_type=jnp.float32
@@ -33,9 +245,28 @@
     return lax.psum_scatter(shares, "wide", scatter_dimension=2, tiled=True)
 
 
+def per_device(wides, narrows, pair_integrals, screening, virtual_integrals, trials):
+    trial_count, orbitals, columns = trials.shape
+    own_i = pair_integrals.shape[0] // orbitals
+    fits = (
+        trial_count == 1
+        and virtual_integrals.shape[0] == 1
+        and screening.shape[1] == wides * narrows
+        and columns == LANES
+        and orbitals % LANES == 0
+        and orbitals % (16 * wides) == 0
+        and narrows % CORES == 0
+        and own_i % 8 == 0
+        and (own_i * orbitals // LANES) % 16 == 0
+    )
+    if fits:
+        return fused(wides, narrows, pair_integrals, screening, virtual_integrals, trials)
+    return plain(pair_integrals, screening, virtual_integrals, trials)
+
+
 def solution(mesh):
     return jax.shard_map(
-        per_device,
+        functools.partial(per_device, mesh.shape["wide"], mesh.shape["narrow"]),
         mesh=mesh,
         in_specs=(
             P(("wide", "narrow"), None),

time: 105 us -> 28.4 us (0.27)
  waiting for transfers between devices: 52.8 us -> 0 us
  blocking collectives: 25.5 us -> 0 us
  Pallas kernels: 0 us -> 23.5 us
  between operations: 13.5 us -> 0.01 us
  starting transfers between devices: 4.96 us -> 0 us
  matrix products: 3.27 us -> 0 us
  other arithmetic: 1.38 us -> 0 us
  local copies, waits for them, and re-layouts: 3.6 us -> 4.65 us
    reduce_scatter x2 -> x0, waiting for transfers between devices: 52.7 us -> none  [the longest x1 29.6 us: per_device(): lax.psum_scatter(jnp.einsum('qasj,ijq->asi', halves, pair_tiles, preferre...]
    pallas_call x0 -> x1, Pallas kernels: none -> 23.5 us  [fused(): pl.pallas_call(functools.partial(kernel, wides, narrows), out_shape=jax.S...]
    all_gather x1 -> x0, blocking collectives: 15.5 us -> none  [per_device(): whole_trials = lax.all_gather(trials, 'narrow', axis=2, tiled=True)]
    all_to_all x1 -> x0, blocking collectives: 9.99 us -> none  [per_device(): lax.all_to_all(blocks, 'wide', split_axis=3, concat_axis=0, tiled=True)]
    all_to_all x1 -> x0, starting transfers between devices: 4.88 us -> none  [per_device(): lax.all_to_all(lax.all_to_all(blocks, 'wide', split_axis=3, concat_axis=0...]
    unnamed x8 -> x9, local copies, waits for them, and re-layouts: 0.88 us -> 4.65 us
    dot_general x2 -> x0, matrix products: 3.27 us -> none  [the longest x1 1.98 us: per_device(): jnp.einsum('qasj,ijq->asi', halves, pair_tiles, preferred_element_type=jn...]
    reduce_scatter x1 -> x0, local copies, waits for them, and re-layouts: 1.64 us -> none  [per_device(): lax.psum_scatter(jnp.einsum('qasj,ijq->asi', halves, pair_tiles, preferre...]
  transfers between devices with their start and end apart: 3 -> 0, of which waited for: 2 -> 0; matrix products, arithmetic and copies ran while one was open for 0% -> 0% of each run, Pallas kernels for 0% -> 0%
where the time goes in v1:
time: 28.4 us; the launch traced here: 28.2 us
  Pallas kernels  23.5 us (83%)
  local copies, waits for them, and re-layouts  4.65 us (16%)
    pallas_call x1, Pallas kernels, fused(): pl.pallas_call(functools.partial(kernel, wides, narrows), out_shape=jax.S...  23.5 us
    unnamed x9, local copies, waits for them, and re-layouts  4.65 us

profile of v1, /device:TPU:0, one launch (start us, length us, event | category | flops | bytes accessed | tf_op | source)
XLA Modules:
  0.0 28.2 jit_solution(14426551504017886221)
XLA Ops:
  0.0 0.0 copy-start
  0.0 1.6 %copy-done = bf16[1,1024,1024]{2,1,0:T(8,128)(2,1)S(1)} copy-done((bf16[1,1024,1024]{2,1,0:T(8,128)(2,1)S(1)}, bf16[1,1024,1024]{2,1,0:T(8,128)(2,1)}, u32[]{:S(2)}) %copy-start) | copy-done | bytes 2097176
  1.6 0.0 copy-start.1
  1.6 0.9 %copy-done.1 = bf16[2048,32]{0,1:T(8,128)(2,1)S(1)} copy-done((bf16[2048,32]{0,1:T(8,128)(2,1)S(1)}, bf16[2048,32]{0,1:T(8,128)(2,1)}, u32[]{:S(2)}) %copy-start.1) | copy-done | bytes 131096
  2.5 0.0 copy-start.2
  2.5 0.8 %copy-done.2 = bf16[1,256,128]{2,1,0:T(8,128)(2,1)S(1)} copy-done((bf16[1,256,128]{2,1,0:T(8,128)(2,1)S(1)}, bf16[1,256,128]{2,1,0:T(8,128)(2,1)}, u32[]{:S(2)}) %copy-start.2) | copy-done | bytes 65560
  3.3 0.0 copy-start.3
  3.3 0.7 %copy-done.3 = bf16[32,32]{1,0:T(8,128)(2,1)S(1)} copy-done((bf16[32,32]{1,0:T(8,128)(2,1)S(1)}, bf16[32,32]{1,0:T(8,128)(2,1)}, u32[]{:S(2)}) %copy-start.3) | copy-done | bytes 2072
  4.0 23.5 %shard_map.46 = f32[64,128]{1,0:T(8,128)S(1)} custom-call(bf16[32,2048]{1,0:T(8,128)(2,1)S(1)} %bitcast.8, bf16[32,32]{1,0:T(8,128)(2,1)S(1)} %copy-done.3, bf16[1024,1024]{1,0:T(8,128)(2,1)S(1)} %bitcast.6, bf16[256,128]{1,0:T(8,128)(2,1)S(1)} %bitcast.9), custom_call_target="tpu_custom_call" | custom-call | tf_op jit(solution)/shard_map/pallas_call | solution.py:187
  27.6 0.6 %copy.6 = f32[128,1,64]{0,2,1:T(8,128)} copy(f32[128,1,64]{0,2,1:T(8,128)S(1)} %bitcast.7) | data formatting | bytes 65536
Async XLA Ops:
  0.0 1.6 %copy-start = (bf16[1,1024,1024]{2,1,0:T(8,128)(2,1)S(1)}, bf16[1,1024,1024]{2,1,0:T(8,128)(2,1)}, u32[]{:S(2)}) copy-start(bf16[1,1024,1024]{2,1,0:T(8,128)(2,1)} %param.6) | copy-start | bytes 6291460
  1.6 0.9 %copy-start.1 = (bf16[2048,32]{0,1:T(8,128)(2,1)S(1)}, bf16[2048,32]{0,1:T(8,128)(2,1)}, u32[]{:S(2)}) copy-start(bf16[2048,32]{0,1:T(8,128)(2,1)} %param.4) | copy-start | bytes 393220
  2.5 0.8 %copy-start.2 = (bf16[1,256,128]{2,1,0:T(8,128)(2,1)S(1)}, bf16[1,256,128]{2,1,0:T(8,128)(2,1)}, u32[]{:S(2)}) copy-start(bf16[1,256,128]{2,1,0:T(8,128)(2,1)} %param.7) | copy-start | bytes 196612
  3.3 0.7 %copy-start.3 = (bf16[32,32]{1,0:T(8,128)(2,1)S(1)}, bf16[32,32]{1,0:T(8,128)(2,1)}, u32[]{:S(2)}) copy-start(bf16[32,32]{1,0:T(8,128)(2,1)} %screen_ref.1) | copy-start | bytes 6148

commit v2 on v1

--- a/solution.py
+++ b/solution.py
@@ -61,6 +61,15 @@
         for k in range(zs)
     ]
 
+    pl.semaphore_wait(barrier, wides + narrows - 2)
+
+    def share(block, of):
+        return trial.at[block, pl.ds(pl.multiple_of(of * cut, cut), cut)]
+
+    mine = trial_ref.at[pl.ds(pl.multiple_of(w * cut, cut), cut)]
+    along_z = {k: send(mine, share(n, w), w, z_at[k] * CORES + c) for k in range(1, zs)}
+    to_mate = send(trial_ref, trial.at[n], w, z * CORES + mate)
+
     get_pairs.wait()
     get_screen.wait()
     product = lax.dot_general(
@@ -76,15 +85,6 @@
             staged[pl.ds(h * own_i + i, aux, stride=rows), :] = product[:, t * LANES : (t + 1) * LANES]
     tiles[...] = staged[...].reshape(tiles.shape).astype(jnp.bfloat16)
     tiles_wide[w] = tiles[w]
-    get_trial.wait()
-
-    pl.semaphore_wait(barrier, wides + narrows - 2)
-
-    def share(block, of):
-        return trial.at[block, pl.ds(pl.multiple_of(of * cut, cut), cut)]
-
-    along_z = {k: send(share(n, w), share(n, w), w, z_at[k] * CORES + c) for k in range(zs - 1, 0, -1)}
-    to_mate = send(trial.at[n], trial.at[n], w, z * CORES + mate)
     tiles_in = [send(tiles.at[wide_at[m]], tiles_wide.at[w], wide_at[m], n) for m in range(1, wides)]
 
     def chunk(k):
@@ -94,6 +94,7 @@
             wide_rows, virt[k], (((1,), (1,)), ((), ())), preferred_element_type=jnp.float32
         )
 
+    get_trial.wait()
     get_virt[0].wait()
     to_mate.wait_recv()
     total[...] = chunk(0)
@@ -117,12 +118,10 @@
             copy.wait_recv()
         block = z_from[k] * CORES + c
         relayed[k] = send(trial.at[block], trial.at[block], w, z * CORES + mate)
-    for k in range(1, zs):
+    for k in range(1, zs - 1):
         get_virt[k].wait()
         relayed[k].wait_recv()
         total[...] += chunk(k)
-    for b in range(narrows):
-        halves[b] = total[:, b * LANES : (b + 1) * LANES].astype(jnp.bfloat16)
 
     for copy in tiles_done:
         copy.wait_recv()
@@ -135,6 +134,12 @@
         ]
         columns.append(jnp.concatenate(parts, axis=0))
     screened = jnp.concatenate(columns, axis=1).astype(jnp.bfloat16)
+
+    get_virt[zs - 1].wait()
+    relayed[zs - 1].wait_recv()
+    whole = (total[...] + chunk(zs - 1)).astype(jnp.bfloat16)
+    for b in range(narrows):
+        halves[b] = whole[:, b * LANES : (b + 1) * LANES]
 
     order = list(range(1, zs)) + [0]
     from_mate, from_wides, from_zs = {}, {}, {}
@@ -212,7 +217,7 @@
             pltpu.SemaphoreType.DMA((copies,)),
         ],
         compiler_params=pltpu.CompilerParams(
-            collective_id=0, has_side_effects=True, vmem_limit_bytes=48 * 2**20
+            collective_id=0, has_side_effects=True, vmem_limit_bytes=60 * 2**20
         ),
     )(pair_integrals.T, screening, virtual_integrals[0], trials[0])
     return out.T[:, None, :]

time: 28.4 us -> 26.1 us (0.919)
  local copies, waits for them, and re-layouts: 4.65 us -> 1.38 us
  Pallas kernels: 23.5 us -> 24.5 us
    unnamed x9 -> x1, local copies, waits for them, and re-layouts: 4.65 us -> 1.38 us
    pallas_call x1, Pallas kernels: 23.5 us -> 24.5 us  [fused(): pl.pallas_call(functools.partial(kernel, wides, narrows), out_shape=jax.S...]
where the time goes in v2:
time: 26.1 us; the launch traced here: 25.9 us
  Pallas kernels  24.5 us (94%)
  local copies, waits for them, and re-layouts  1.38 us (5%)
    pallas_call x1, Pallas kernels, fused(): pl.pallas_call(functools.partial(kernel, wides, narrows), out_shape=jax.S...  24.5 us
    unnamed x1, local copies, waits for them, and re-layouts  1.38 us

profile of v2, /device:TPU:0, one launch (start us, length us, event | category | flops | bytes accessed | tf_op | source)
XLA Modules:
  0.0 25.9 jit_solution(13613041900767443830)
XLA Ops:
  0.0 24.5 %shard_map.46 = f32[64,128]{1,0:T(8,128)} custom-call(bf16[32,2048]{1,0:T(8,128)(2,1)} %bitcast.8, bf16[32,32]{1,0:T(8,128)(2,1)} %screen_ref.1, bf16[1024,1024]{1,0:T(8,128)(2,1)} %bitcast.6, bf16[256,128]{1,0:T(8,128)(2,1)} %bitcast.9), custom_call_target="tpu_custom_call" | custom-call | tf_op jit(solution)/shard_map/pallas_call | solution.py:192
  24.6 1.4 %copy.6 = f32[128,1,64]{0,2,1:T(8,128)} copy(f32[128,1,64]{0,2,1:T(8,128)} %bitcast.7) | data formatting | bytes 65536

commit v3 on v2

--- a/solution.py
+++ b/solution.py
@@ -10,6 +10,16 @@
 LANES = 128
 CORES = 2
 MESH = pl.DeviceIdType.MESH
+
+
+def flipped(index, mask):
+    bit = 1
+    result = index
+    while bit <= mask:
+        if mask & bit:
+            result = result + bit * (1 - 2 * lax.rem(lax.div(index, bit), 2))
+        bit *= 2
+    return result
 
 
 def kernel(
@@ -24,10 +34,10 @@
     mate = 1 - c
     orbitals = trial.shape[1]
     cut = orbitals // wides
-    wide_at = [lax.rem(w + m, wides) for m in range(wides)]
-    z_at = [lax.rem(z + k, zs) for k in range(zs)]
-    z_from = [lax.rem(z + zs - k, zs) for k in range(zs)]
-    narrow_at = [lax.rem(n + m, narrows) for m in range(narrows)]
+    wide_at = [flipped(w, m) for m in range(wides)]
+    z_at = [flipped(z, k) for k in range(zs)]
+    narrow_at = [flipped(n, m) for m in range(narrows)]
+    wide_order = [wides - 1] + list(range(1, wides - 1))
 
     barrier = pltpu.get_barrier_semaphore()
     for m in range(1, wides):
@@ -57,7 +67,7 @@
     get_trial = fetch(trial_ref, trial.at[n], 2)
     depth = virt.shape[2]
     get_virt = [
-        fetch(virt_ref.at[:, pl.ds(pl.multiple_of(z_from[k] * depth, depth), depth)], virt.at[k], 3 + k)
+        fetch(virt_ref.at[:, pl.ds(pl.multiple_of(z_at[k] * depth, depth), depth)], virt.at[k], 3 + k)
         for k in range(zs)
     ]
 
@@ -85,10 +95,10 @@
             staged[pl.ds(h * own_i + i, aux, stride=rows), :] = product[:, t * LANES : (t + 1) * LANES]
     tiles[...] = staged[...].reshape(tiles.shape).astype(jnp.bfloat16)
     tiles_wide[w] = tiles[w]
-    tiles_in = [send(tiles.at[wide_at[m]], tiles_wide.at[w], wide_at[m], n) for m in range(1, wides)]
+    tiles_in = [send(tiles.at[wide_at[m]], tiles_wide.at[w], wide_at[m], n) for m in wide_order]
 
     def chunk(k):
-        first = z_from[k] * CORES
+        first = z_at[k] * CORES
         wide_rows = jnp.concatenate([trial[first + p] for p in range(CORES)], axis=1)
         return lax.dot_general(
             wide_rows, virt[k], (((1,), (1,)), ((), ())), preferred_element_type=jnp.float32
@@ -102,8 +112,8 @@
     across = {}
     for k in range(1, zs):
         along_z[k].wait_recv()
-        block = z_from[k] * CORES + c
-        across[k] = [send(share(block, w), share(block, w), wide_at[m], n) for m in range(1, wides)]
+        block = z_at[k] * CORES + c
+        across[k] = [send(share(block, w), share(block, w), wide_at[m], n) for m in wide_order]
 
     for copy in tiles_in:
         copy.wait_recv()
@@ -116,7 +126,7 @@
     for k in range(1, zs):
         for copy in across[k]:
             copy.wait_recv()
-        block = z_from[k] * CORES + c
+        block = z_at[k] * CORES + c
         relayed[k] = send(trial.at[block], trial.at[block], w, z * CORES + mate)
     for k in range(1, zs - 1):
         get_virt[k].wait()
@@ -141,13 +151,14 @@
     for b in range(narrows):
         halves[b] = whole[:, b * LANES : (b + 1) * LANES]
 
-    order = list(range(1, zs)) + [0]
+    order = list(range(zs - 1, -1, -1))
     from_mate, from_wides, from_zs = {}, {}, {}
     for k in order:
         to_core[k] = jnp.dot(
             screened, halves[z_at[k] * CORES + mate], preferred_element_type=jnp.float32
         ).astype(jnp.bfloat16)
         from_mate[k] = send(to_core.at[k], from_core.at[k], w, z * CORES + mate)
+    early = len(sent)
     for k in order:
         own = jnp.dot(screened, halves[z_at[k] * CORES + c], preferred_element_type=jnp.float32)
         from_mate[k].wait_recv()
@@ -159,21 +170,26 @@
                 to_wide.at[k, pl.ds(pl.multiple_of(wide_at[m] * cut, cut), cut)],
                 from_wide.at[k, m - 1], wide_at[m], n,
             )
-            for m in range(1, wides)
+            for m in wide_order
         ]
+    for copy in sent[:early]:
+        copy.wait_send()
     for k in order:
         value = summed[k, pl.ds(pl.multiple_of(w * cut, cut), cut), :]
+        for copy in from_wides[k]:
+            copy.wait_recv()
         for m in range(1, wides):
-            from_wides[k][m - 1].wait_recv()
             value = value + from_wide[k, m - 1].astype(jnp.float32)
         if k:
             to_z[k - 1] = value.astype(jnp.bfloat16)
             from_zs[k] = send(to_z.at[k - 1], from_z.at[k - 1], w, z_at[k] * CORES + c)
+    for copy in sent[early : early + zs * (wides - 1)]:
+        copy.wait_send()
     for k in range(1, zs):
         from_zs[k].wait_recv()
         value = value + from_z[k - 1].astype(jnp.float32)
     out_ref[...] = value
-    for copy in sent:
+    for copy in sent[early + zs * (wides - 1) :]:
         copy.wait_send()
 
 
@@ -189,6 +205,7 @@
     copies = (zs - 1) * 2 + 1 + (zs - 1) * (wides - 1) + (wides - 1) + (narrows - 1)
     copies += zs + zs * (wides - 1) + (zs - 1)
     anywhere = pl.BlockSpec(memory_space=pl.ANY)
+    operands = (pair_integrals.T, screening, virtual_integrals[0], trials[0])
     out = pl.pallas_call(
         functools.partial(kernel, wides, narrows),
         out_shape=jax.ShapeDtypeStruct((cut, columns), f4),
@@ -217,9 +234,9 @@
             pltpu.SemaphoreType.DMA((copies,)),
         ],
         compiler_params=pltpu.CompilerParams(
-            collective_id=0, has_side_effects=True, vmem_limit_bytes=60 * 2**20
+            collective_id=0, has_side_effects=True, vmem_limit_bytes=32 * 2**20
         ),
-    )(pair_integrals.T, screening, virtual_integrals[0], trials[0])
+    )(*[pltpu.with_memory_space_constraint(x, pltpu.HBM) for x in operands])
     return out.T[:, None, :]
 
 
@@ -261,6 +278,10 @@
         and orbitals % LANES == 0
         and orbitals % (16 * wides) == 0
         and narrows % CORES == 0
+        and wides & (wides - 1) == 0
+        and narrows & (narrows - 1) == 0
+        and wides > 1
+        and narrows > CORES
         and own_i % 8 == 0
         and (own_i * orbitals // LANES) % 16 == 0
     )

time: 26.1 us -> 24.7 us (0.946)
  local copies, waits for them, and re-layouts: 1.38 us -> 0.62 us
  Pallas kernels: 24.5 us -> 23.9 us
    unnamed x1, local copies, waits for them, and re-layouts: 1.38 us -> 0.62 us
    pallas_call x1, Pallas kernels: 24.5 us -> 23.9 us  [fused(): pl.pallas_call(functools.partial(kernel, wides, narrows), out_shape=jax.S...]
where the time goes in v3:
time: 24.7 us; the launch traced here: 24.5 us
  Pallas kernels  23.9 us (97%)
  local copies, waits for them, and re-layouts  0.62 us (3%)
    pallas_call x1, Pallas kernels, fused(): pl.pallas_call(functools.partial(kernel, wides, narrows), out_shape=jax.S...  23.9 us
    unnamed x1, local copies, waits for them, and re-layouts  0.62 us

profile of v3, /device:TPU:0, one launch (start us, length us, event | category | flops | bytes accessed | tf_op | source)
XLA Modules:
  0.0 24.5 jit_solution(9209723727693248786)
XLA Ops:
  0.0 23.9 %shard_map.46 = f32[64,128]{1,0:T(8,128)S(1)} custom-call(bf16[32,2048]{1,0:T(8,128)(2,1)} %bitcast.8, bf16[32,32]{1,0:T(8,128)(2,1)} %screen_ref.1, bf16[1024,1024]{1,0:T(8,128)(2,1)} %bitcast.7, bf16[256,128]{1,0:T(8,128)(2,1)} %bitcast.9), custom_call_target="tpu_custom_call" | custom-call | tf_op jit(solution)/shard_map/pallas_call | solution.py:209
  23.9 0.6 %copy.6 = f32[128,1,64]{0,2,1:T(8,128)} copy(f32[128,1,64]{0,2,1:T(8,128)S(1)} %bitcast.6) | data formatting | bytes 65536

commit v4 on v3

--- a/solution.py
+++ b/solution.py
@@ -24,7 +24,7 @@
 
 def kernel(
     wides, narrows, pairs_ref, screen_ref, virt_ref, trial_ref, out_ref,
-    pairs, screen, virt, trial, staged, tiles, tiles_wide, tiles_all, total, halves,
+    pairs, screen, virt, trial, staged, tiles, tiles_wide, tiles_all, total, partial,
     to_core, from_core, summed, to_wide, from_wide, to_z, from_z,
     local_sem, send_sem, recv_sem,
 ):
@@ -148,21 +148,22 @@
     get_virt[zs - 1].wait()
     relayed[zs - 1].wait_recv()
     whole = (total[...] + chunk(zs - 1)).astype(jnp.bfloat16)
+
+    product = jnp.dot(screened, whole, preferred_element_type=jnp.float32)
     for b in range(narrows):
-        halves[b] = whole[:, b * LANES : (b + 1) * LANES]
-
+        to_core[b] = product[:, b * LANES : (b + 1) * LANES].astype(jnp.bfloat16)
     order = list(range(zs - 1, -1, -1))
     from_mate, from_wides, from_zs = {}, {}, {}
     for k in order:
-        to_core[k] = jnp.dot(
-            screened, halves[z_at[k] * CORES + mate], preferred_element_type=jnp.float32
-        ).astype(jnp.bfloat16)
-        from_mate[k] = send(to_core.at[k], from_core.at[k], w, z * CORES + mate)
+        from_mate[k] = send(
+            to_core.at[z_at[k] * CORES + mate], from_core.at[k], w, z * CORES + mate
+        )
+    for b in range(narrows):
+        partial[b] = product[:, b * LANES : (b + 1) * LANES]
     early = len(sent)
     for k in order:
-        own = jnp.dot(screened, halves[z_at[k] * CORES + c], preferred_element_type=jnp.float32)
         from_mate[k].wait_recv()
-        value = own + from_core[k].astype(jnp.float32)
+        value = partial[z_at[k] * CORES + c] + from_core[k].astype(jnp.float32)
         summed[k] = value
         to_wide[k] = value.astype(jnp.bfloat16)
         from_wides[k] = [
@@ -221,8 +222,8 @@
             pltpu.VMEM((wides, narrows, rows, LANES), bf),
             pltpu.VMEM((narrows, wides, rows, LANES), bf),
             pltpu.VMEM((orbitals, virtuals), f4),
+            pltpu.VMEM((narrows, orbitals, columns), f4),
             pltpu.VMEM((narrows, orbitals, columns), bf),
-            pltpu.VMEM((zs, orbitals, columns), bf),
             pltpu.VMEM((zs, orbitals, columns), bf),
             pltpu.VMEM((zs, orbitals, columns), f4),
             pltpu.VMEM((zs, orbitals, columns), bf),

time: 24.7 us -> 24.5 us (level)
  no operation moved by 1% of the time
where the time goes in v4:
time: 24.5 us; the launch traced here: 24.3 us
  Pallas kernels  23.7 us (97%)
  local copies, waits for them, and re-layouts  0.62 us (3%)
    pallas_call x1, Pallas kernels, fused(): pl.pallas_call(functools.partial(kernel, wides, narrows), out_shape=jax.S...  23.7 us
    unnamed x1, local copies, waits for them, and re-layouts  0.62 us

profile of v4, /device:TPU:0, one launch (start us, length us, event | category | flops | bytes accessed | tf_op | source)
XLA Modules:
  0.0 24.3 jit_solution(11575418878723849318)
XLA Ops:
  0.0 23.7 %shard_map.46 = f32[64,128]{1,0:T(8,128)S(1)} custom-call(bf16[32,2048]{1,0:T(8,128)(2,1)} %bitcast.8, bf16[32,32]{1,0:T(8,128)(2,1)} %screen_ref.1, bf16[1024,1024]{1,0:T(8,128)(2,1)} %bitcast.7, bf16[256,128]{1,0:T(8,128)(2,1)} %bitcast.9), custom_call_target="tpu_custom_call" | custom-call | tf_op jit(solution)/shard_map/pallas_call | solution.py:210
  23.7 0.6 %copy.6 = f32[128,1,64]{0,2,1:T(8,128)} copy(f32[128,1,64]{0,2,1:T(8,128)S(1)} %bitcast.6) | data formatting | bytes 65536

commit v5 on v4

--- a/solution.py
+++ b/solution.py
@@ -62,23 +62,23 @@
         copy.start()
         return copy
 
+    get_trial = fetch(trial_ref, trial.at[n], 2)
     get_pairs = fetch(pairs_ref, pairs, 0)
     get_screen = fetch(screen_ref, screen, 1)
-    get_trial = fetch(trial_ref, trial.at[n], 2)
+
+    pl.semaphore_wait(barrier, wides + narrows - 2)
+
+    def share(block, of):
+        return trial.at[block, pl.ds(pl.multiple_of(of * cut, cut), cut)]
+
+    get_trial.wait()
+    along_z = {k: send(share(n, w), share(n, w), w, z_at[k] * CORES + c) for k in range(1, zs)}
+    to_mate = send(trial.at[n], trial.at[n], w, z * CORES + mate)
     depth = virt.shape[2]
     get_virt = [
         fetch(virt_ref.at[:, pl.ds(pl.multiple_of(z_at[k] * depth, depth), depth)], virt.at[k], 3 + k)
         for k in range(zs)
     ]
-
-    pl.semaphore_wait(barrier, wides + narrows - 2)
-
-    def share(block, of):
-        return trial.at[block, pl.ds(pl.multiple_of(of * cut, cut), cut)]
-
-    mine = trial_ref.at[pl.ds(pl.multiple_of(w * cut, cut), cut)]
-    along_z = {k: send(mine, share(n, w), w, z_at[k] * CORES + c) for k in range(1, zs)}
-    to_mate = send(trial_ref, trial.at[n], w, z * CORES + mate)
 
     get_pairs.wait()
     get_screen.wait()
@@ -104,7 +104,6 @@
             wide_rows, virt[k], (((1,), (1,)), ((), ())), preferred_element_type=jnp.float32
         )
 
-    get_trial.wait()
     get_virt[0].wait()
     to_mate.wait_recv()
     total[...] = chunk(0)
@@ -119,7 +118,8 @@
         copy.wait_recv()
     tiles_all[n] = tiles_wide[:, n]
     tiles_done = [
-        send(tiles_wide.at[:, narrow_at[m]], tiles_all.at[n], w, narrow_at[m]) for m in range(1, narrows)
+        send(tiles_wide.at[:, narrow_at[m]], tiles_all.at[n], w, narrow_at[m])
+        for m in range(narrows - 1, 0, -1)
     ]
 
     relayed = {}
@@ -133,6 +133,8 @@
         relayed[k].wait_recv()
         total[...] += chunk(k)
 
+    get_virt[zs - 1].wait()
+    relayed[zs - 1].wait_recv()
     for copy in tiles_done:
         copy.wait_recv()
     columns = []
@@ -145,8 +147,6 @@
         columns.append(jnp.concatenate(parts, axis=0))
     screened = jnp.concatenate(columns, axis=1).astype(jnp.bfloat16)
 
-    get_virt[zs - 1].wait()
-    relayed[zs - 1].wait_recv()
     whole = (total[...] + chunk(zs - 1)).astype(jnp.bfloat16)
 
     product = jnp.dot(screened, whole, preferred_element_type=jnp.float32)

time: 24.5 us -> 24.4 us (level)
  no operation moved by 1% of the time
where the time goes in v5:
time: 24.4 us; the launch traced here: 24.2 us
  Pallas kernels  23.6 us (97%)
  local copies, waits for them, and re-layouts  0.62 us (3%)
    pallas_call x1, Pallas kernels, fused(): pl.pallas_call(functools.partial(kernel, wides, narrows), out_shape=jax.S...  23.6 us
    unnamed x1, local copies, waits for them, and re-layouts  0.62 us

profile of v5, /device:TPU:0, one launch (start us, length us, event | category | flops | bytes accessed | tf_op | source)
XLA Modules:
  0.0 24.2 jit_solution(9314363461488366330)
XLA Ops:
  0.0 23.6 %shard_map.46 = f32[64,128]{1,0:T(8,128)S(1)} custom-call(bf16[32,2048]{1,0:T(8,128)(2,1)} %bitcast.8, bf16[32,32]{1,0:T(8,128)(2,1)} %screen_ref.1, bf16[1024,1024]{1,0:T(8,128)(2,1)} %bitcast.7, bf16[256,128]{1,0:T(8,128)(2,1)} %bitcast.9), custom_call_target="tpu_custom_call" | custom-call | tf_op jit(solution)/shard_map/pallas_call | solution.py:210
  23.6 0.6 %copy.6 = f32[128,1,64]{0,2,1:T(8,128)} copy(f32[128,1,64]{0,2,1:T(8,128)S(1)} %bitcast.6) | data formatting | bytes 65536

commit v6 on v5

--- a/solution.py
+++ b/solution.py
@@ -24,8 +24,8 @@
 
 def kernel(
     wides, narrows, pairs_ref, screen_ref, virt_ref, trial_ref, out_ref,
-    pairs, screen, virt, trial, staged, tiles, tiles_wide, tiles_all, total, partial,
-    to_core, from_core, summed, to_wide, from_wide, to_z, from_z,
+    pairs, screen, virt, trial, staged, tiles, tiles_all, total,
+    summed, to_wide, from_wide, to_z, from_z,
     local_sem, send_sem, recv_sem,
 ):
     zs = narrows // CORES
@@ -36,14 +36,17 @@
     cut = orbitals // wides
     wide_at = [flipped(w, m) for m in range(wides)]
     z_at = [flipped(z, k) for k in range(zs)]
-    narrow_at = [flipped(n, m) for m in range(narrows)]
     wide_order = [wides - 1] + list(range(1, wides - 1))
+    order = list(range(zs - 1, -1, -1))
+    peers = [(m, k) for k in order for m in wide_order + [0] if m or k]
 
     barrier = pltpu.get_barrier_semaphore()
-    for m in range(1, wides):
-        pl.semaphore_signal(barrier, inc=1, device_id={"wide": wide_at[m], "narrow": n}, device_id_type=MESH)
-    for m in range(1, narrows):
-        pl.semaphore_signal(barrier, inc=1, device_id={"wide": w, "narrow": narrow_at[m]}, device_id_type=MESH)
+    for m, k in peers:
+        peer = {"wide": wide_at[m], "narrow": z_at[k] * CORES + c}
+        pl.semaphore_signal(barrier, inc=1, device_id=peer, device_id_type=MESH)
+    pl.semaphore_signal(
+        barrier, inc=1, device_id={"wide": w, "narrow": z * CORES + mate}, device_id_type=MESH
+    )
 
     sent = []
 
@@ -57,6 +60,9 @@
         sent.append(copy)
         return copy
 
+    def to_mate(source, target):
+        return send(source, target, w, z * CORES + mate)
+
     def fetch(source, target, at):
         copy = pltpu.make_async_copy(source, target, local_sem.at[at])
         copy.start()
@@ -66,19 +72,22 @@
     get_pairs = fetch(pairs_ref, pairs, 0)
     get_screen = fetch(screen_ref, screen, 1)
 
-    pl.semaphore_wait(barrier, wides + narrows - 2)
+    pl.semaphore_wait(barrier, len(peers) + 1)
 
     def share(block, of):
         return trial.at[block, pl.ds(pl.multiple_of(of * cut, cut), cut)]
 
     get_trial.wait()
     along_z = {k: send(share(n, w), share(n, w), w, z_at[k] * CORES + c) for k in range(1, zs)}
-    to_mate = send(trial.at[n], trial.at[n], w, z * CORES + mate)
-    depth = virt.shape[2]
-    get_virt = [
-        fetch(virt_ref.at[:, pl.ds(pl.multiple_of(z_at[k] * depth, depth), depth)], virt.at[k], 3 + k)
-        for k in range(zs)
-    ]
+    own_block = to_mate(trial.at[n], trial.at[n])
+
+    depth = virt.shape[4]
+
+    def rows_for(core, k):
+        return virt_ref.at[:, core, :, pl.ds(pl.multiple_of(z_at[k] * depth, depth), depth)]
+
+    get_virt = [fetch(rows_for(c, k), virt.at[k, c], 3 + k) for k in range(zs)]
+    mate_virt = [to_mate(rows_for(mate, k), virt.at[k, c]) for k in range(zs)]
 
     get_pairs.wait()
     get_screen.wait()
@@ -94,19 +103,19 @@
             t = i * halves_j + h
             staged[pl.ds(h * own_i + i, aux, stride=rows), :] = product[:, t * LANES : (t + 1) * LANES]
     tiles[...] = staged[...].reshape(tiles.shape).astype(jnp.bfloat16)
-    tiles_wide[w] = tiles[w]
-    tiles_in = [send(tiles.at[wide_at[m]], tiles_wide.at[w], wide_at[m], n) for m in wide_order]
+    tiles_in = {k: [] for k in order}
+    for m, k in peers:
+        source = tiles.at[wide_at[m], pl.ds(z_at[k] * CORES, CORES)]
+        tiles_in[k].append(send(source, tiles_all.at[c, w, z], wide_at[m], z_at[k] * CORES + c))
+    tiles_all[c, w, z] = tiles[w, pl.ds(z * CORES, CORES)]
 
     def chunk(k):
         first = z_at[k] * CORES
         wide_rows = jnp.concatenate([trial[first + p] for p in range(CORES)], axis=1)
         return lax.dot_general(
-            wide_rows, virt[k], (((1,), (1,)), ((), ())), preferred_element_type=jnp.float32
+            wide_rows, virt[k].reshape(-1, depth), (((1,), (1,)), ((), ())),
+            preferred_element_type=jnp.float32,
         )
-
-    get_virt[0].wait()
-    to_mate.wait_recv()
-    total[...] = chunk(0)
 
     across = {}
     for k in range(1, zs):
@@ -114,69 +123,72 @@
         block = z_at[k] * CORES + c
         across[k] = [send(share(block, w), share(block, w), wide_at[m], n) for m in wide_order]
 
-    for copy in tiles_in:
-        copy.wait_recv()
-    tiles_all[n] = tiles_wide[:, n]
-    tiles_done = [
-        send(tiles_wide.at[:, narrow_at[m]], tiles_all.at[n], w, narrow_at[m])
-        for m in range(narrows - 1, 0, -1)
-    ]
-
-    relayed = {}
+    get_virt[0].wait()
+    own_block.wait_recv()
+    mate_virt[0].wait_recv()
+    total[...] = chunk(0)
+
+    relayed, tiles_done = {}, []
+
+    def relay_tiles(k):
+        for copy in tiles_in[k]:
+            copy.wait_recv()
+        group = tiles_all.at[c, :, z_at[k]]
+        tiles_done.append(to_mate(group, group))
+
     for k in range(1, zs):
+        relay_tiles(zs - k)
         for copy in across[k]:
             copy.wait_recv()
         block = z_at[k] * CORES + c
-        relayed[k] = send(trial.at[block], trial.at[block], w, z * CORES + mate)
-    for k in range(1, zs - 1):
+        relayed[k] = to_mate(trial.at[block], trial.at[block])
+    relay_tiles(0)
+    for k in range(1, zs):
         get_virt[k].wait()
+        mate_virt[k].wait_recv()
         relayed[k].wait_recv()
-        total[...] += chunk(k)
-
-    get_virt[zs - 1].wait()
-    relayed[zs - 1].wait_recv()
+        if k < zs - 1:
+            total[...] += chunk(k)
     for copy in tiles_done:
         copy.wait_recv()
-    columns = []
-    for h in range(halves_j):
-        parts = [
-            tiles_all[b, a].astype(jnp.float32)[h * own_i : (h + 1) * own_i]
-            for a in range(wides)
-            for b in range(narrows)
-        ]
-        columns.append(jnp.concatenate(parts, axis=0))
-    screened = jnp.concatenate(columns, axis=1).astype(jnp.bfloat16)
+
+    def screened(q):
+        columns = []
+        for h in range(halves_j):
+            parts = [
+                tiles_all[p, a, b, q].astype(jnp.float32)[h * own_i : (h + 1) * own_i]
+                for a in range(wides)
+                for b in range(zs)
+                for p in range(CORES)
+            ]
+            columns.append(jnp.concatenate(parts, axis=0))
+        return jnp.concatenate(columns, axis=1).astype(jnp.bfloat16)
 
     whole = (total[...] + chunk(zs - 1)).astype(jnp.bfloat16)
 
-    product = jnp.dot(screened, whole, preferred_element_type=jnp.float32)
-    for b in range(narrows):
-        to_core[b] = product[:, b * LANES : (b + 1) * LANES].astype(jnp.bfloat16)
-    order = list(range(zs - 1, -1, -1))
-    from_mate, from_wides, from_zs = {}, {}, {}
-    for k in order:
-        from_mate[k] = send(
-            to_core.at[z_at[k] * CORES + mate], from_core.at[k], w, z * CORES + mate
-        )
-    for b in range(narrows):
-        partial[b] = product[:, b * LANES : (b + 1) * LANES]
+    span = zs * LANES
+    product = sum(
+        jnp.dot(screened(q), whole[:, q * span : (q + 1) * span], preferred_element_type=jnp.float32)
+        for q in range(CORES)
+    )
+    for b in range(zs):
+        to_wide[b] = product[:, b * LANES : (b + 1) * LANES].astype(jnp.bfloat16)
+    from_wides, from_zs = {}, {}
     early = len(sent)
     for k in order:
-        from_mate[k].wait_recv()
-        value = partial[z_at[k] * CORES + c] + from_core[k].astype(jnp.float32)
-        summed[k] = value
-        to_wide[k] = value.astype(jnp.bfloat16)
         from_wides[k] = [
             send(
-                to_wide.at[k, pl.ds(pl.multiple_of(wide_at[m] * cut, cut), cut)],
+                to_wide.at[z_at[k], pl.ds(pl.multiple_of(wide_at[m] * cut, cut), cut)],
                 from_wide.at[k, m - 1], wide_at[m], n,
             )
             for m in wide_order
         ]
+    for b in range(zs):
+        summed[b] = product[:, b * LANES : (b + 1) * LANES]
     for copy in sent[:early]:
         copy.wait_send()
     for k in order:
-        value = summed[k, pl.ds(pl.multiple_of(w * cut, cut), cut), :]
+        value = summed[z_at[k], pl.ds(pl.multiple_of(w * cut, cut), cut), :]
         for copy in from_wides[k]:
             copy.wait_recv()
         for m in range(1, wides):
@@ -203,10 +215,11 @@
     rows = pairs_here // LANES
     cut = orbitals // wides
     bf, f4 = jnp.bfloat16, jnp.float32
-    copies = (zs - 1) * 2 + 1 + (zs - 1) * (wides - 1) + (wides - 1) + (narrows - 1)
-    copies += zs + zs * (wides - 1) + (zs - 1)
+    copies = (zs - 1) * 2 + 1 + zs + (wides * zs - 1) + (zs - 1) * (wides - 1) + zs
+    copies += zs * (wides - 1) + (zs - 1)
     anywhere = pl.BlockSpec(memory_space=pl.ANY)
-    operands = (pair_integrals.T, screening, virtual_integrals[0], trials[0])
+    slabs = virtual_integrals.reshape(zs, CORES, columns, virtuals)
+    operands = (pair_integrals.T, screening, slabs, trials[0])
     out = pl.pallas_call(
         functools.partial(kernel, wides, narrows),
         out_shape=jax.ShapeDtypeStruct((cut, columns), f4),
@@ -215,16 +228,12 @@
         scratch_shapes=[
             pltpu.VMEM((aux, pairs_here), bf),
             pltpu.VMEM(screening.shape, bf),
-            pltpu.VMEM((zs, virtuals, virtuals // zs), bf),
+            pltpu.VMEM((zs, CORES, zs, columns, virtuals // zs), bf),
             pltpu.VMEM((narrows, orbitals, columns), bf),
             pltpu.VMEM((aux * rows, LANES), f4),
             pltpu.VMEM((wides, narrows, rows, LANES), bf),
-            pltpu.VMEM((wides, narrows, rows, LANES), bf),
-            pltpu.VMEM((narrows, wides, rows, LANES), bf),
+            pltpu.VMEM((CORES, wides, zs, CORES, rows, LANES), bf),
             pltpu.VMEM((orbitals, virtuals), f4),
-            pltpu.VMEM((narrows, orbitals, columns), f4),
-            pltpu.VMEM((narrows, orbitals, columns), bf),
-            pltpu.VMEM((zs, orbitals, columns), bf),
             pltpu.VMEM((zs, orbitals, columns), f4),
             pltpu.VMEM((zs, orbitals, columns), bf),
             pltpu.VMEM((zs, wides - 1, cut, columns), bf),

time: 24.4 us -> 24.5 us (level)
  no operation moved by 1% of the time
where the time goes in v6:
time: 24.5 us; the launch traced here: 24.3 us
  Pallas kernels  23.7 us (97%)
  local copies, waits for them, and re-layouts  0.62 us (3%)
    pallas_call x1, Pallas kernels, fused(): pl.pallas_call(functools.partial(kernel, wides, narrows), out_shape=jax.S...  23.7 us
    unnamed x1, local copies, waits for them, and re-layouts  0.62 us

profile of v6, /device:TPU:0, one launch (start us, length us, event | category | flops | bytes accessed | tf_op | source)
XLA Modules:
  0.0 24.3 jit_solution(18197490713394519158)
XLA Ops:
  0.0 23.7 %shard_map.46 = f32[64,128]{1,0:T(8,128)S(1)} custom-call(bf16[32,2048]{1,0:T(8,128)(2,1)} %bitcast.8, bf16[32,32]{1,0:T(8,128)(2,1)} %screen_ref.1, bf16[4,2,128,1024]{3,2,1,0:T(8,128)(2,1)} %bitcast.7, bf16[256,128]{1,0:T(8,128)(2,1)} %bitcast.9), custom_call_target="tpu_custom_call" | custom-call | tf_op jit(solution)/shard_map/pallas_call | solution.py:223
  23.7 0.6 %copy.6 = f32[128,1,64]{0,2,1:T(8,128)} copy(f32[128,1,64]{0,2,1:T(8,128)S(1)} %bitcast.6) | data formatting | bytes 65536

commit v7 on v6

--- a/solution.py
+++ b/solution.py
@@ -24,7 +24,7 @@
 
 def kernel(
     wides, narrows, pairs_ref, screen_ref, virt_ref, trial_ref, out_ref,
-    pairs, screen, virt, trial, staged, tiles, tiles_all, total,
+    pairs, screen, virt, trial, staged, tiles, tiles_all, screened, total,
     summed, to_wide, from_wide, to_z, from_z,
     local_sem, send_sem, recv_sem,
 ):
@@ -128,13 +128,28 @@
     mate_virt[0].wait_recv()
     total[...] = chunk(0)
 
-    relayed, tiles_done = {}, []
+    relayed, tiles_done = {}, {}
 
     def relay_tiles(k):
         for copy in tiles_in[k]:
             copy.wait_recv()
         group = tiles_all.at[c, :, z_at[k]]
-        tiles_done.append(to_mate(group, group))
+        tiles_done[k] = to_mate(group, group)
+
+    def assemble(k):
+        tall = CORES * own_i
+        for a in range(wides):
+            at = pl.ds(pl.multiple_of((a * zs + z_at[k]) * tall, tall), tall)
+            for q in range(CORES):
+                parts = [tiles_all[p, a, z_at[k], q].astype(jnp.float32) for p in range(CORES)]
+                for h in range(halves_j):
+                    both = jnp.concatenate([part[h * own_i : (h + 1) * own_i] for part in parts], axis=0)
+                    screened[q, at, h * LANES : (h + 1) * LANES] = both.astype(jnp.bfloat16)
+
+    def arrive(k):
+        get_virt[k].wait()
+        mate_virt[k].wait_recv()
+        relayed[k].wait_recv()
 
     for k in range(1, zs):
         relay_tiles(zs - k)
@@ -142,33 +157,23 @@
             copy.wait_recv()
         block = z_at[k] * CORES + c
         relayed[k] = to_mate(trial.at[block], trial.at[block])
-    relay_tiles(0)
-    for k in range(1, zs):
-        get_virt[k].wait()
-        mate_virt[k].wait_recv()
-        relayed[k].wait_recv()
-        if k < zs - 1:
-            total[...] += chunk(k)
-    for copy in tiles_done:
-        copy.wait_recv()
-
-    def screened(q):
-        columns = []
-        for h in range(halves_j):
-            parts = [
-                tiles_all[p, a, b, q].astype(jnp.float32)[h * own_i : (h + 1) * own_i]
-                for a in range(wides)
-                for b in range(zs)
-                for p in range(CORES)
-            ]
-            columns.append(jnp.concatenate(parts, axis=0))
-        return jnp.concatenate(columns, axis=1).astype(jnp.bfloat16)
-
+        if k == zs - 1:
+            relay_tiles(0)
+        if k > 1:
+            arrive(k - 1)
+            tiles_done[zs - k + 1].wait_recv()
+            total[...] += chunk(k - 1)
+            assemble(zs - k + 1)
+    tiles_done[1].wait_recv()
+    assemble(1)
+    tiles_done[0].wait_recv()
+    arrive(zs - 1)
+    assemble(0)
     whole = (total[...] + chunk(zs - 1)).astype(jnp.bfloat16)
 
     span = zs * LANES
     product = sum(
-        jnp.dot(screened(q), whole[:, q * span : (q + 1) * span], preferred_element_type=jnp.float32)
+        jnp.dot(screened[q], whole[:, q * span : (q + 1) * span], preferred_element_type=jnp.float32)
         for q in range(CORES)
     )
     for b in range(zs):
@@ -233,6 +238,7 @@
             pltpu.VMEM((aux * rows, LANES), f4),
             pltpu.VMEM((wides, narrows, rows, LANES), bf),
             pltpu.VMEM((CORES, wides, zs, CORES, rows, LANES), bf),
+            pltpu.VMEM((CORES, orbitals, orbitals), bf),
             pltpu.VMEM((orbitals, virtuals), f4),
             pltpu.VMEM((zs, orbitals, columns), f4),
             pltpu.VMEM((zs, orbitals, columns), bf),

time: 24.5 us -> 24.8 us (1.012)
  Pallas kernels: 23.7 us -> 24 us
    pallas_call x1, Pallas kernels: 23.7 us -> 24 us  [fused(): pl.pallas_call(functools.partial(kernel, wides, narrows), out_shape=jax.S...]
where the time goes in v7:
time: 24.8 us; the launch traced here: 24.6 us
  Pallas kernels  24 us (97%)
  local copies, waits for them, and re-layouts  0.62 us (2%)
    pallas_call x1, Pallas kernels, fused(): pl.pallas_call(functools.partial(kernel, wides, narrows), out_shape=jax.S...  24 us
    unnamed x1, local copies, waits for them, and re-layouts  0.62 us

profile of v7, /device:TPU:0, one launch (start us, length us, event | category | flops | bytes accessed | tf_op | source)
XLA Modules:
  0.0 24.6 jit_solution(9567785243551059160)
XLA Ops:
  0.0 24.0 %shard_map.46 = f32[64,128]{1,0:T(8,128)S(1)} custom-call(bf16[32,2048]{1,0:T(8,128)(2,1)} %bitcast.8, bf16[32,32]{1,0:T(8,128)(2,1)} %screen_ref.1, bf16[4,2,128,1024]{3,2,1,0:T(8,128)(2,1)} %bitcast.7, bf16[256,128]{1,0:T(8,128)(2,1)} %bitcast.9), custom_call_target="tpu_custom_call" | custom-call | tf_op jit(solution)/shard_map/pallas_call | solution.py:228
  24.0 0.6 %copy.6 = f32[128,1,64]{0,2,1:T(8,128)} copy(f32[128,1,64]{0,2,1:T(8,128)S(1)} %bitcast.6) | data formatting | bytes 65536

commit v8 on v5

--- a/solution.py
+++ b/solution.py
@@ -24,7 +24,7 @@
 
 def kernel(
     wides, narrows, pairs_ref, screen_ref, virt_ref, trial_ref, out_ref,
-    pairs, screen, virt, trial, staged, tiles, tiles_wide, tiles_all, total, partial,
+    pairs, screen, virt, trial, staged, tiles, tiles_all, total, partial,
     to_core, from_core, summed, to_wide, from_wide, to_z, from_z,
     local_sem, send_sem, recv_sem,
 ):
@@ -40,10 +40,10 @@
     wide_order = [wides - 1] + list(range(1, wides - 1))
 
     barrier = pltpu.get_barrier_semaphore()
-    for m in range(1, wides):
-        pl.semaphore_signal(barrier, inc=1, device_id={"wide": wide_at[m], "narrow": n}, device_id_type=MESH)
-    for m in range(1, narrows):
-        pl.semaphore_signal(barrier, inc=1, device_id={"wide": w, "narrow": narrow_at[m]}, device_id_type=MESH)
+    peers = [(m, k) for k in range(narrows - 1, -1, -1) for m in wide_order + [0] if m or k]
+    for m, k in peers:
+        peer = {"wide": wide_at[m], "narrow": narrow_at[k]}
+        pl.semaphore_signal(barrier, inc=1, device_id=peer, device_id_type=MESH)
 
     sent = []
 
@@ -66,7 +66,7 @@
     get_pairs = fetch(pairs_ref, pairs, 0)
     get_screen = fetch(screen_ref, screen, 1)
 
-    pl.semaphore_wait(barrier, wides + narrows - 2)
+    pl.semaphore_wait(barrier, len(peers))
 
     def share(block, of):
         return trial.at[block, pl.ds(pl.multiple_of(of * cut, cut), cut)]
@@ -94,8 +94,11 @@
             t = i * halves_j + h
             staged[pl.ds(h * own_i + i, aux, stride=rows), :] = product[:, t * LANES : (t + 1) * LANES]
     tiles[...] = staged[...].reshape(tiles.shape).astype(jnp.bfloat16)
-    tiles_wide[w] = tiles[w]
-    tiles_in = [send(tiles.at[wide_at[m]], tiles_wide.at[w], wide_at[m], n) for m in wide_order]
+    tiles_done = [
+        send(tiles.at[wide_at[m], narrow_at[k]], tiles_all.at[n, w], wide_at[m], narrow_at[k])
+        for m, k in peers
+    ]
+    tiles_all[n, w] = tiles[w, n]
 
     def chunk(k):
         first = z_at[k] * CORES
@@ -104,23 +107,15 @@
             wide_rows, virt[k], (((1,), (1,)), ((), ())), preferred_element_type=jnp.float32
         )
 
-    get_virt[0].wait()
-    to_mate.wait_recv()
-    total[...] = chunk(0)
-
     across = {}
     for k in range(1, zs):
         along_z[k].wait_recv()
         block = z_at[k] * CORES + c
         across[k] = [send(share(block, w), share(block, w), wide_at[m], n) for m in wide_order]
 
-    for copy in tiles_in:
-        copy.wait_recv()
-    tiles_all[n] = tiles_wide[:, n]
-    tiles_done = [
-        send(tiles_wide.at[:, narrow_at[m]], tiles_all.at[n], w, narrow_at[m])
-        for m in range(narrows - 1, 0, -1)
-    ]
+    get_virt[0].wait()
+    to_mate.wait_recv()
+    total[...] = chunk(0)
 
     relayed = {}
     for k in range(1, zs):
@@ -203,7 +198,7 @@
     rows = pairs_here // LANES
     cut = orbitals // wides
     bf, f4 = jnp.bfloat16, jnp.float32
-    copies = (zs - 1) * 2 + 1 + (zs - 1) * (wides - 1) + (wides - 1) + (narrows - 1)
+    copies = (zs - 1) * 2 + 1 + (zs - 1) * (wides - 1) + (wides * narrows - 1)
     copies += zs + zs * (wides - 1) + (zs - 1)
     anywhere = pl.BlockSpec(memory_space=pl.ANY)
     operands = (pair_integrals.T, screening, virtual_integrals[0], trials[0])
@@ -218,7 +213,6 @@
             pltpu.VMEM((zs, virtuals, virtuals // zs), bf),
             pltpu.VMEM((narrows, orbitals, columns), bf),
             pltpu.VMEM((aux * rows, LANES), f4),
-            pltpu.VMEM((wides, narrows, rows, LANES), bf),
             pltpu.VMEM((wides, narrows, rows, LANES), bf),
             pltpu.VMEM((narrows, wides, rows, LANES), bf),
             pltpu.VMEM((orbitals, virtuals), f4),

time: 24.4 us -> 26.4 us (1.082)
  Pallas kernels: 23.6 us -> 25.6 us
    pallas_call x1, Pallas kernels: 23.6 us -> 25.6 us  [fused(): pl.pallas_call(functools.partial(kernel, wides, narrows), out_shape=jax.S...]
where the time goes in v8:
time: 26.4 us; the launch traced here: 26.3 us
  Pallas kernels  25.6 us (97%)
  local copies, waits for them, and re-layouts  0.62 us (2%)
    pallas_call x1, Pallas kernels, fused(): pl.pallas_call(functools.partial(kernel, wides, narrows), out_shape=jax.S...  25.6 us
    unnamed x1, local copies, waits for them, and re-layouts  0.62 us

profile of v8, /device:TPU:0, one launch (start us, length us, event | category | flops | bytes accessed | tf_op | source)
XLA Modules:
  0.0 26.3 jit_solution(7322665878472855793)
XLA Ops:
  0.0 25.6 %shard_map.46 = f32[64,128]{1,0:T(8,128)S(1)} custom-call(bf16[32,2048]{1,0:T(8,128)(2,1)} %bitcast.8, bf16[32,32]{1,0:T(8,128)(2,1)} %screen_ref.1, bf16[1024,1024]{1,0:T(8,128)(2,1)} %bitcast.7, bf16[256,128]{1,0:T(8,128)(2,1)} %bitcast.9), custom_call_target="tpu_custom_call" | custom-call | tf_op jit(solution)/shard_map/pallas_call | solution.py:205
  25.6 0.6 %copy.6 = f32[128,1,64]{0,2,1:T(8,128)} copy(f32[128,1,64]{0,2,1:T(8,128)S(1)} %bitcast.6) | data formatting | bytes 65536

commit v9 on v7

--- a/solution.py
+++ b/solution.py
@@ -24,7 +24,7 @@
 
 def kernel(
     wides, narrows, pairs_ref, screen_ref, virt_ref, trial_ref, out_ref,
-    pairs, screen, virt, trial, staged, tiles, tiles_all, screened, total,
+    pairs, screen, virt, trial, staged, tiles, tiles_wide, tiles_all, screened, total,
     summed, to_wide, from_wide, to_z, from_z,
     local_sem, send_sem, recv_sem,
 ):
@@ -38,15 +38,12 @@
     z_at = [flipped(z, k) for k in range(zs)]
     wide_order = [wides - 1] + list(range(1, wides - 1))
     order = list(range(zs - 1, -1, -1))
-    peers = [(m, k) for k in order for m in wide_order + [0] if m or k]
 
     barrier = pltpu.get_barrier_semaphore()
-    for m, k in peers:
-        peer = {"wide": wide_at[m], "narrow": z_at[k] * CORES + c}
-        pl.semaphore_signal(barrier, inc=1, device_id=peer, device_id_type=MESH)
-    pl.semaphore_signal(
-        barrier, inc=1, device_id={"wide": w, "narrow": z * CORES + mate}, device_id_type=MESH
-    )
+    for m in wide_order:
+        pl.semaphore_signal(barrier, inc=1, device_id={"wide": wide_at[m], "narrow": n}, device_id_type=MESH)
+    for narrow in [z_at[k] * CORES + c for k in range(1, zs)] + [z * CORES + mate]:
+        pl.semaphore_signal(barrier, inc=1, device_id={"wide": w, "narrow": narrow}, device_id_type=MESH)
 
     sent = []
 
@@ -72,7 +69,7 @@
     get_pairs = fetch(pairs_ref, pairs, 0)
     get_screen = fetch(screen_ref, screen, 1)
 
-    pl.semaphore_wait(barrier, len(peers) + 1)
+    pl.semaphore_wait(barrier, wides - 1 + zs)
 
     def share(block, of):
         return trial.at[block, pl.ds(pl.multiple_of(of * cut, cut), cut)]
@@ -103,11 +100,8 @@
             t = i * halves_j + h
             staged[pl.ds(h * own_i + i, aux, stride=rows), :] = product[:, t * LANES : (t + 1) * LANES]
     tiles[...] = staged[...].reshape(tiles.shape).astype(jnp.bfloat16)
-    tiles_in = {k: [] for k in order}
-    for m, k in peers:
-        source = tiles.at[wide_at[m], pl.ds(z_at[k] * CORES, CORES)]
-        tiles_in[k].append(send(source, tiles_all.at[c, w, z], wide_at[m], z_at[k] * CORES + c))
-    tiles_all[c, w, z] = tiles[w, pl.ds(z * CORES, CORES)]
+    tiles_wide[w] = tiles[w]
+    tiles_in = [send(tiles.at[wide_at[m]], tiles_wide.at[w], wide_at[m], n) for m in wide_order]
 
     def chunk(k):
         first = z_at[k] * CORES
@@ -123,6 +117,14 @@
         block = z_at[k] * CORES + c
         across[k] = [send(share(block, w), share(block, w), wide_at[m], n) for m in wide_order]
 
+    for copy in tiles_in:
+        copy.wait_recv()
+    tiles_z = {}
+    for k in range(zs - 1, 0, -1):
+        source = tiles_wide.at[:, pl.ds(z_at[k] * CORES, CORES)]
+        tiles_z[k] = send(source, tiles_all.at[c, :, z], w, z_at[k] * CORES + c)
+    tiles_all[c, :, z] = tiles_wide[:, pl.ds(z * CORES, CORES)]
+
     get_virt[0].wait()
     own_block.wait_recv()
     mate_virt[0].wait_recv()
@@ -131,8 +133,8 @@
     relayed, tiles_done = {}, {}
 
     def relay_tiles(k):
-        for copy in tiles_in[k]:
-            copy.wait_recv()
+        if k:
+            tiles_z[k].wait_recv()
         group = tiles_all.at[c, :, z_at[k]]
         tiles_done[k] = to_mate(group, group)
 
@@ -220,7 +222,7 @@
     rows = pairs_here // LANES
     cut = orbitals // wides
     bf, f4 = jnp.bfloat16, jnp.float32
-    copies = (zs - 1) * 2 + 1 + zs + (wides * zs - 1) + (zs - 1) * (wides - 1) + zs
+    copies = (zs - 1) * 2 + 1 + zs + (wides - 1) + (zs - 1) + (zs - 1) * (wides - 1) + zs
     copies += zs * (wides - 1) + (zs - 1)
     anywhere = pl.BlockSpec(memory_space=pl.ANY)
     slabs = virtual_integrals.reshape(zs, CORES, columns, virtuals)
@@ -236,6 +238,7 @@
             pltpu.VMEM((zs, CORES, zs, columns, virtuals // zs), bf),
             pltpu.VMEM((narrows, orbitals, columns), bf),
             pltpu.VMEM((aux * rows, LANES), f4),
+            pltpu.VMEM((wides, narrows, rows, LANES), bf),
             pltpu.VMEM((wides, narrows, rows, LANES), bf),
             pltpu.VMEM((CORES, wides, zs, CORES, rows, LANES), bf),
             pltpu.VMEM((CORES, orbitals, orbitals), bf),

time: 24.8 us -> 25.3 us (1.020)
  Pallas kernels: 24 us -> 24.6 us
    pallas_call x1, Pallas kernels: 24 us -> 24.6 us  [fused(): pl.pallas_call(functools.partial(kernel, wides, narrows), out_shape=jax.S...]
where the time goes in v9:
time: 25.3 us; the launch traced here: 25.2 us
  Pallas kernels  24.6 us (97%)
  local copies, waits for them, and re-layouts  0.62 us (2%)
    pallas_call x1, Pallas kernels, fused(): pl.pallas_call(functools.partial(kernel, wides, narrows), out_shape=jax.S...  24.6 us
    unnamed x1, local copies, waits for them, and re-layouts  0.62 us

profile of v9, /device:TPU:0, one launch (start us, length us, event | category | flops | bytes accessed | tf_op | source)
XLA Modules:
  0.0 25.2 jit_solution(3565740533439652660)
XLA Ops:
  0.0 24.6 %shard_map.46 = f32[64,128]{1,0:T(8,128)S(1)} custom-call(bf16[32,2048]{1,0:T(8,128)(2,1)} %bitcast.8, bf16[32,32]{1,0:T(8,128)(2,1)} %screen_ref.1, bf16[4,2,128,1024]{3,2,1,0:T(8,128)(2,1)} %bitcast.7, bf16[256,128]{1,0:T(8,128)(2,1)} %bitcast.9), custom_call_target="tpu_custom_call" | custom-call | tf_op jit(solution)/shard_map/pallas_call | solution.py:230
  24.6 0.6 %copy.6 = f32[128,1,64]{0,2,1:T(8,128)} copy(f32[128,1,64]{0,2,1:T(8,128)S(1)} %bitcast.6) | data formatting | bytes 65536

commit v10 on v5

--- a/solution.py
+++ b/solution.py
@@ -104,16 +104,6 @@
             wide_rows, virt[k], (((1,), (1,)), ((), ())), preferred_element_type=jnp.float32
         )
 
-    get_virt[0].wait()
-    to_mate.wait_recv()
-    total[...] = chunk(0)
-
-    across = {}
-    for k in range(1, zs):
-        along_z[k].wait_recv()
-        block = z_at[k] * CORES + c
-        across[k] = [send(share(block, w), share(block, w), wide_at[m], n) for m in wide_order]
-
     for copy in tiles_in:
         copy.wait_recv()
     tiles_all[n] = tiles_wide[:, n]
@@ -121,6 +111,16 @@
         send(tiles_wide.at[:, narrow_at[m]], tiles_all.at[n], w, narrow_at[m])
         for m in range(narrows - 1, 0, -1)
     ]
+
+    across = {}
+    for k in range(1, zs):
+        along_z[k].wait_recv()
+        block = z_at[k] * CORES + c
+        across[k] = [send(share(block, w), share(block, w), wide_at[m], n) for m in wide_order]
+
+    get_virt[0].wait()
+    to_mate.wait_recv()
+    total[...] = chunk(0)
 
     relayed = {}
     for k in range(1, zs):

time: 24.4 us -> 24.6 us (level)
  no operation moved by 1% of the time
where the time goes in v10:
time: 24.6 us; the launch traced here: 24.4 us
  Pallas kernels  23.8 us (97%)
  local copies, waits for them, and re-layouts  0.62 us (3%)
    pallas_call x1, Pallas kernels, fused(): pl.pallas_call(functools.partial(kernel, wides, narrows), out_shape=jax.S...  23.8 us
    unnamed x1, local copies, waits for them, and re-layouts  0.62 us

profile of v10, /device:TPU:0, one launch (start us, length us, event | category | flops | bytes accessed | tf_op | source)
XLA Modules:
  0.0 24.4 jit_solution(3703992532573978393)
XLA Ops:
  0.0 23.8 %shard_map.46 = f32[64,128]{1,0:T(8,128)S(1)} custom-call(bf16[32,2048]{1,0:T(8,128)(2,1)} %bitcast.8, bf16[32,32]{1,0:T(8,128)(2,1)} %screen_ref.1, bf16[1024,1024]{1,0:T(8,128)(2,1)} %bitcast.7, bf16[256,128]{1,0:T(8,128)(2,1)} %bitcast.9), custom_call_target="tpu_custom_call" | custom-call | tf_op jit(solution)/shard_map/pallas_call | solution.py:210
  23.8 0.6 %copy.6 = f32[128,1,64]{0,2,1:T(8,128)} copy(f32[128,1,64]{0,2,1:T(8,128)S(1)} %bitcast.6) | data formatting | bytes 65536
